TPU v7x, 128 devices: a whole 4x4x4 slice. The times are simulated.
128 devices in a mesh: sib: 2 (over x_lo), row: 8 (over y, core), col: 8 (over z, x_hi).
Axes of the slice: x: 4 (x_hi: 2, x_lo: 2; x = x_hi * 2 + x_lo), y: 4, z: 4, core: 2. Of those that a mesh axis runs over, the one named last changes fastest.
Arguments:
- child_tiles: float32 [2, 64, 128, 128, 128], P('sib', ('row', 'col')), may hold values from -6 to 6
- child_rows: int32 [2, 64], P('sib'), may hold values from 0 to 127, as said below
- child_slots: int32 [2, 64, 128], P('sib', ('row', 'col')), may hold values from 0 to 4095, as said below
- tile_count: int32 [2, 64], P('sib', ('row', 'col')), may hold values from 64 to 128, as said below
- inverses: float32 [2, 512, 512], replicated, as said below
Outputs:
- factored: float32 [8, 16, 16, 8, 128, 128], P(None, ('sib', 'row'), None, 'col')
Inputs may be any that keep to these rules, and one draw needn't show every extreme that they name: `child_rows`: A child's entries are distinct; entry i leaves the same remainder as i when divided by the number of grid rows of the parent. `child_slots`: call the owner of parent tile (I, J) the grid row I mod (number of grid rows) and grid column J mod (number of grid columns). Among the live slots of one device at most 2 carry tiles with one owner; in every draw some device reaches 2 for some owner. `tile_count`: some device of each child has all 128 slots live. `inverses`: each matrix is lower triangular with positive diagonal.
All inputs are finite; a program needn't handle non-finite values.
Results may differ from a plain program's by a relative error of at most 0.00012.
Values sent between devices are 32-bit elements; how exact they have to be, the bound alone decides.
No kernel may reach another device: no remote copies, remote signals or barrier semaphores. Data moves between devices by JAX's collectives and lax.ppermute only.
A program may use at most 192 MiB of HBM per device.

v0:
```python
import jax
import jax.numpy as jnp
from jax import lax
from jax.sharding import PartitionSpec as P

NF = 16384
TILE = 128
PANEL = 512
NPANEL = 2
CHILD_TILES = 64
CAP = 2


def broadcast(value, axis, source):
    kept = jnp.where(lax.axis_index(axis) == source, value, 0).astype(value.dtype)
    return lax.psum(kept, axis)


def local(child_tiles, child_rows, child_slots, tile_count, inverses):
    grid_rows = lax.axis_size("sib") * lax.axis_size("row")
    columns = lax.axis_size("col")
    devices = grid_rows * columns
    tile_order = NF // TILE
    local_rows = tile_order // grid_rows
    local_cols = tile_order // columns
    tile_data = child_tiles[0, 0]
    slot_ids = child_slots[0, 0]
    live_count = tile_count[0, 0]
    row_list = child_rows[0]
    slot_total = slot_ids.shape[0]
    child_row = slot_ids // CHILD_TILES
    child_col = slot_ids % CHILD_TILES
    positions = jnp.arange(CHILD_TILES, dtype=jnp.int32)
    parent_row = jnp.sum(
        jnp.where(child_row[:, None] == positions[None, :], row_list[None, :], 0), axis=1
    )
    parent_col = jnp.sum(
        jnp.where(child_col[:, None] == positions[None, :], row_list[None, :], 0), axis=1
    )
    owner_index = parent_row % grid_rows * columns + parent_col % columns
    target = parent_row // grid_rows * local_cols + parent_col // columns
    slot_order = jnp.arange(slot_total, dtype=jnp.int32)
    is_live = slot_order < live_count
    earlier = (
        (owner_index[:, None] == owner_index[None, :])
        & is_live[None, :]
        & (slot_order[None, :] < slot_order[:, None])
    )
    slot_rank = jnp.sum(earlier.astype(jnp.int32), axis=1)
    slot_place = jnp.where(is_live, owner_index * CAP + slot_rank, devices * CAP)
    outgoing = (
        jnp.zeros((devices * CAP, TILE, TILE), jnp.float32)
        .at[slot_place]
        .set(tile_data, mode="drop")
    )
    destined = jnp.zeros((devices * CAP,), jnp.int32).at[slot_place].set(target, mode="drop")
    arrived, landing = (
        lax.all_to_all(
            outgoing.reshape(devices, CAP, TILE, TILE),
            ("sib", "row", "col"),
            split_axis=0,
            concat_axis=0,
            tiled=True,
        ),
        lax.all_to_all(
            destined.reshape(devices, CAP),
            ("sib", "row", "col"),
            split_axis=0,
            concat_axis=0,
            tiled=True,
        ),
    )
    front_tiles = jnp.zeros((local_rows * local_cols, TILE, TILE), jnp.float32)
    front_tiles = front_tiles.at[landing.reshape(-1)].add(arrived.reshape(-1, TILE, TILE))
    front_tiles = front_tiles.reshape(local_rows, local_cols, TILE, TILE)
    my_row = lax.axis_index(("sib", "row"))
    my_col = lax.axis_index("col")
    panel_tiles = PANEL // TILE
    root_count = grid_rows // columns
    tile_ids = jnp.arange(local_rows, dtype=jnp.int32) * grid_rows + my_row
    for panel_step in range(NPANEL):
        first_tile = panel_tiles * panel_step
        below_tile = first_tile + panel_tiles
        column_slot = first_tile // columns
        start_col = first_tile % columns
        is_below = tile_ids >= below_tile
        weights = inverses[panel_step]
        column_block = front_tiles[:, column_slot]
        holds_panel = (my_col >= start_col) & (my_col < start_col + panel_tiles)
        offset = jnp.clip(my_col - start_col, 0, panel_tiles - 1)
        everyone = lax.all_gather(column_block[None], "col", axis=0, tiled=True)
        chosen = everyone[start_col : start_col + panel_tiles]
        panel_rows = chosen.transpose(1, 2, 0, 3).reshape(local_rows * TILE, PANEL)
        factor = jnp.dot(panel_rows, weights.T, precision=lax.Precision.HIGHEST)
        factor = (
            factor.reshape(local_rows, TILE, PANEL) * is_below.astype(jnp.float32)[:, None, None]
        )
        panel_piece = lax.dynamic_slice_in_dim(factor, offset * TILE, TILE, 2)
        replace = is_below[:, None, None] & holds_panel
        front_tiles = front_tiles.at[:, column_slot].set(
            jnp.where(replace, panel_piece, column_block)
        )
        received = [
            broadcast(factor, ("sib", "row"), root_step * columns + my_col)
            for root_step in range(root_count)
        ]
        column_factor = jnp.stack(received, 1).reshape(local_cols, TILE, PANEL)
        front_tiles = front_tiles - jnp.einsum(
            "aip,bjp->abij", factor, column_factor, precision=lax.Precision.HIGHEST
        )
    return front_tiles.reshape(local_rows, 1, local_cols, 1, TILE, TILE)


def solution(mesh):
    return jax.shard_map(
        local,
        mesh=mesh,
        in_specs=(
            P("sib", ("row", "col"), None, None, None),
            P("sib", None),
            P("sib", ("row", "col"), None),
            P("sib", ("row", "col")),
            P(),
        ),
        out_specs=P(None, ("sib", "row"), None, "col", None, None),
        check_vma=False,
    )
```

profile of v0, /device:TPU:0, one launch (start us, length us, event | category | flops | bytes accessed | tf_op | source)
XLA Modules:
  0.0 837.8 jit_solution(17602744139437200190)
XLA Ops:
  6.5 0.7 and_select_fusion.7
  7.9 0.7 select_reduce_fusion
  8.6 0.2 convert_reduce_fusion
  8.8 1.0 scatter_custom_fusion
  9.8 0.8 all_to_all.9
  10.6 11.1 %all-to-all-start = ((s32[128,1,2]{2,1,0:T(1,128)}), s32[128,1,2]{2,1,0:T(1,128)S(1)}, u32[]{:S(2)}, u32[]{:S(2)}) async-start(s32[128,1,2]{2,1,0:T(1,128)} %bitcast.7), calls=%async_computation | async-start | bytes 131072 | tf_op jit(solution)/shard_map/all_to_all | solution.py:65
  21.7 7.9 broadcast_in_dim.69
  29.6 23.2 %scatter_fusion = f32[256,128,128]{2,1,0:T(8,128)} fusion(f32[256,128,128]{2,1,0:T(8,128)} %broadcast_in_dim.69, s32[128]{0:T(128)S(1)} %fusion.16, f32[128,128,128]{2,1,0:T(8,128)} %bitcast.120), kind=kCustom, calls=%fused_computation.1 | custom fusion | bytes 25166336 | tf_op jit(solution)/shard_map/scatter | solution.py:54
  52.8 0.0 all-to-all-done
  52.8 10.2 %all-to-all-start.1 = ((f32[128,2,128,128]{3,2,1,0:T(8,128)}), f32[128,2,128,128]{3,2,1,0:T(8,128)}, u32[]{:S(2)}, u32[]{:S(2)}) async-start(f32[128,2,128,128]{3,2,1,0:T(8,128)} %bitcast.117), calls=%async_computation.1 | async-start | bytes 33554432 | tf_op jit(solution)/shard_map/all_to_all | solution.py:58
  63.0 0.0 all-gather.5.cloned.1.call-start
  63.1 0.5 broadcast.445
  63.6 0.8 reduce.7
  64.4 0.1 reshape.347
  64.6 222.0 %all-to-all-done.1 = f32[128,2,128,128]{3,2,1,0:T(8,128)} async-done(((f32[128,2,128,128]{3,2,1,0:T(8,128)}), f32[128,2,128,128]{3,2,1,0:T(8,128)}, u32[]{:S(2)}, u32[]{:S(2)}) %all-to-all-start.1) | async-done | bytes 16777248 | tf_op jit(solution)/shard_map/all_to_all | solution.py:58
  286.6 4.5 broadcast_in_dim.64
  291.0 51.2 %scatter_fusion.1 = f32[128,128,128]{2,1,0:T(8,128)} fusion(f32[128,128,128]{2,1,0:T(8,128)} %broadcast_in_dim.64, s32[256]{0:T(256)S(1)} %bitcast.125, f32[256,128,128]{2,1,0:T(8,128)} %bitcast.11), kind=kCustom, calls=%fused_computation.2 | custom fusion | flops 4194304 | bytes 50332672 | tf_op jit(solution)/shard_map/scatter-add | solution.py:74
  342.2 1.9 slice_bitcast_fusion.1
  344.1 0.0 all-gather.5.cloned.1.call-update
  344.2 0.0 all-reduce.7.cloned.1.call-start
  344.3 85.3 %all-gather.5.cloned.1.call-done = f32[64,1,128,128]{3,2,1,0:T(8,128)} async-done(((f32[8,1,128,128]{3,2,1,0:T(8,128)}), f32[64,1,128,128]{3,2,1,0:T(8,128)}) %all-gather.5.cloned.1.call-update) | async-done | bytes 4194320 | tf_op jit(solution)/shard_map/all_gather | solution.py:91
  429.5 0.0 slice-start.2
  429.5 1.6 slice-done.2
  431.1 1.4 copy.53
  432.5 1.9 dot_general.16
  434.4 5.3 convolution_multiply_fusion.1
  439.7 2.6 select_bitcast_fusion.3
  442.3 0.0 all-reduce.7.cloned.1.call-update
  442.3 0.5 all-gather.7.cloned.1.call-start
  442.8 7.7 copy.36
  450.5 0.9 bitcast_dynamic-update-slice_fusion.1
  451.4 118.5 %all-reduce.7.cloned.1.call-done = (f32[8,1,128,512]{3,2,0,1:T(8,128)}, f32[8,1,128,512]{3,2,0,1:T(8,128)}) async-done(((f32[8,1,128,512]{3,2,0,1:T(8,128)}, f32[8,1,128,512]{3,2,0,1:T(8,128)}), (f32[8,1,128,512]{3,2,0,1:T(8,128)}, f32[8,1,128,512]{3,2,0,1:T(8,128)})) %all-reduce.7.cloned.1.call-update) | async-done | bytes 4194320 | tf_op jit(solution)/shard_map/psum | solution.py:16
  570.0 2.9 pad_maximum_fusion
  572.9 0.6 copy.37
  573.5 15.8 %bitcast_subtract_fusion.1 = f32[8,16,128,128]{3,2,0,1:T(8,128)S(1)} fusion(f32[8,16,128,128]{3,2,0,1:T(8,128)} %bitcast_dynamic-update-slice_fusion.1, f32[16,128,512,1]{2,1,3,0:T(8,128)S(1)} %bitcast.118, f32[8,128,512]{2,1,0:T(8,128)S(1)} %convolution_multiply_fusion.1), kind=kOutput, calls=%fused_computation.5 | convolution fusion | flops 12886999040 | bytes 23068672 | tf_op jit(solution)/shard_map/aip,bjp->abij/dot_general | solution.py:108
  589.4 0.0 copy-start
  589.4 3.4 copy-done
  592.8 0.9 slice_bitcast_fusion
  593.7 0.0 all-gather.7.cloned.1.call-update
  593.7 0.0 all-reduce.5.cloned.1.call-start
  593.8 72.4 %all-gather.7.cloned.1.call-done = f32[64,1,128,128]{3,2,1,0:T(8,128)} async-done(((f32[8,1,128,128]{3,2,1,0:T(8,128)}), f32[64,1,128,128]{3,2,1,0:T(8,128)}) %all-gather.7.cloned.1.call-update) | async-done | bytes 4194320 | tf_op jit(solution)/shard_map/all_gather | solution.py:91
  666.1 0.0 slice-start.3
  666.1 1.6 slice-done.3
  667.7 1.4 copy.52
  669.1 2.0 dot_general.19
  671.1 5.3 convolution_multiply_fusion
  676.4 2.6 select_bitcast_fusion.1
  679.1 0.0 all-reduce.5.cloned.1.call-update
  679.1 0.9 bitcast_dynamic-update-slice_fusion
  680.0 126.6 %all-reduce.5.cloned.1.call-done = (f32[8,1,128,512]{3,2,0,1:T(8,128)}, f32[8,1,128,512]{3,2,0,1:T(8,128)}) async-done(((f32[8,1,128,512]{3,2,0,1:T(8,128)}, f32[8,1,128,512]{3,2,0,1:T(8,128)}), (f32[8,1,128,512]{3,2,0,1:T(8,128)}, f32[8,1,128,512]{3,2,0,1:T(8,128)})) %all-reduce.5.cloned.1.call-update) | async-done | bytes 4194320 | tf_op jit(solution)/shard_map/psum | solution.py:16
  806.6 0.0 slice-start
  806.6 3.1 pad_maximum_fusion.1
  809.7 0.0 slice-start.1
  809.7 0.6 copy.41
  810.3 0.0 slice-done
  810.3 1.7 slice-done.1
  812.0 15.0 %fusion = f32[8,1,16,1,128,128]{5,4,0,2,3,1:T(8,128)S(1)} fusion(f32[8,16,128,128]{3,2,0,1:T(8,128)S(1)} %bitcast.116, f32[16,128,512,1]{2,1,3,0:T(8,128)S(1)} %bitcast.119, f32[8,128,512]{2,1,0:T(8,128)S(1)} %convolution_multiply_fusion), kind=kOutput, calls=%fused_computation.4 | convolution fusion | flops 12886999040 | bytes 23068672 | tf_op jit(solution)/shard_map/aip,bjp->abij/dot_general | solution.py:108
  827.0 4.0 copy.43
  (7 shorter events, 0.1 us)
Async XLA Ops:
  10.6 42.2 %all-to-all-start = ((s32[128,1,2]{2,1,0:T(1,128)}), s32[128,1,2]{2,1,0:T(1,128)S(1)}, u32[]{:S(2)}, u32[]{:S(2)}) async-start(s32[128,1,2]{2,1,0:T(1,128)} %bitcast.7), calls=%async_computation | async-start | bytes 131072 | tf_op jit(solution)/shard_map/all_to_all | solution.py:65
  52.8 233.7 %all-to-all-start.1 = ((f32[128,2,128,128]{3,2,1,0:T(8,128)}), f32[128,2,128,128]{3,2,1,0:T(8,128)}, u32[]{:S(2)}, u32[]{:S(2)}) async-start(f32[128,2,128,128]{3,2,1,0:T(8,128)} %bitcast.117), calls=%async_computation.1 | async-start | bytes 33554432 | tf_op jit(solution)/shard_map/all_to_all | solution.py:58
  63.0 366.5 %all-gather.5.cloned.1.call-start = ((), (), s32[]{:S(2)}) async-start(), calls=%async_computation.2 | async-start | bytes 4718592 | tf_op jit(solution)/shard_map/all_gather | solution.py:91
  344.2 225.8 %all-reduce.7.cloned.1.call-start = ((), (), s32[]{:S(2)}) async-start(), calls=%async_computation.5 | async-start | bytes 8388608 | tf_op jit(solution)/shard_map/psum | solution.py:16
  429.5 1.6 slice-start.2
  442.3 223.9 %all-gather.7.cloned.1.call-start = ((), (), s32[]{:S(2)}) async-start(), calls=%async_computation.3 | async-start | bytes 4718592 | tf_op jit(solution)/shard_map/all_gather | solution.py:91
  589.4 3.4 copy-start
  593.7 212.9 %all-reduce.5.cloned.1.call-start = ((), (), s32[]{:S(2)}) async-start(), calls=%async_computation.4 | async-start | bytes 8388608 | tf_op jit(solution)/shard_map/psum | solution.py:16
  666.1 1.6 slice-start.3
  806.6 3.7 slice-start
  809.7 2.3 slice-start.1
Sparse Core Ops, SparseCore 0:
  344.3 85.1 all-gather.4
  442.4 127.5 all-reduce.6
  593.8 72.2 all-gather.6
  679.2 127.3 all-reduce.4
where the time goes:
time: 847 us; the launch traced here: 838 us
  waiting for transfers between devices  625 us (74%)
  local copies, waits for them, and re-layouts  68.5 us (8%)
  other arithmetic  66.7 us (8%)
  matrix products  41.5 us (5%)
  starting transfers between devices  22 us (3%)
  between operations  14.2 us (2%)
    psum x2, waiting for transfers between devices, broadcast(): return lax.psum(kept, axis)  245 us
    all_to_all x1, waiting for transfers between devices, local(): lax.all_to_all(outgoing.reshape(devices, CAP, TILE, TILE), ('sib', 'row',...  222 us
    all_gather x2, waiting for transfers between devices, local(): everyone = lax.all_gather(column_block[None], 'col', axis=0, tiled=True)  158 us
    scatter-add x1, other arithmetic, local(): front_tiles.at[landing.reshape(-1)].add(arrived.reshape(-1, TILE, TILE))  51.2 us
    dot_general x2, matrix products, local(): jnp.einsum('aip,bjp->abij', factor, column_factor, precision=lax.Precisio...  30.9 us
    scatter x1, local copies, waits for them, and re-layouts, local(): outgoing = jnp.zeros((devices * CAP, TILE, TILE), jnp.float32).at[slot_pl...  23.2 us
  transfers between devices with their start and end apart: 6, of which 5 were waited for; matrix products, arithmetic and copies ran while one was open for 5% of the time, Pallas kernels for 0%

commit v1 on v0

--- a/solution.py
+++ b/solution.py
@@ -13,7 +13,7 @@
 
 def broadcast(value, axis, source):
     kept = jnp.where(lax.axis_index(axis) == source, value, 0).astype(value.dtype)
-    return lax.psum(kept, axis)
+    return jnp.sum(lax.all_gather(kept, axis), axis=0)
 
 
 def local(child_tiles, child_rows, child_slots, tile_count, inverses):

time: 847 us -> 1300 us (1.53)
  waiting for transfers between devices: 625 us -> 1010 us
  other arithmetic: 66.7 us -> 117 us
    all_gather x0 -> x4, waiting for transfers between devices: none -> 633 us  [broadcast(): return jnp.sum(lax.all_gather(kept, axis), axis=0)]
    psum x2 -> x0, waiting for transfers between devices: 245 us -> none  [broadcast(): return lax.psum(kept, axis)]
    reduce_sum x0 -> x4, other arithmetic: none -> 56.5 us  [broadcast(): return jnp.sum(lax.all_gather(kept, axis), axis=0)]
  transfers between devices with their start and end apart: 6 -> 8, of which waited for: 5 -> 7; matrix products, arithmetic and copies ran while one was open for 5% -> 5% of each run, Pallas kernels for 0% -> 0%
where the time goes in v1:
time: 1300 us; the launch traced here: 1290 us
  waiting for transfers between devices  1010 us (78%)
  other arithmetic  117 us (9%)
  local copies, waits for them, and re-layouts  67.6 us (5%)
  matrix products  46.6 us (4%)
  starting transfers between devices  33.7 us (3%)
  between operations  14.7 us (1%)
    all_gather x4, waiting for transfers between devices, broadcast(): return jnp.sum(lax.all_gather(kept, axis), axis=0)  633 us
    all_to_all x1, waiting for transfers between devices, local(): lax.all_to_all(outgoing.reshape(devices, CAP, TILE, TILE), ('sib', 'row',...  222 us
    all_gather x2, waiting for transfers between devices, local(): everyone = lax.all_gather(column_block[None], 'col', axis=0, tiled=True)  158 us
    reduce_sum x4, other arithmetic, broadcast(): return jnp.sum(lax.all_gather(kept, axis), axis=0)  56.5 us
    scatter-add x1, other arithmetic, local(): front_tiles.at[landing.reshape(-1)].add(arrived.reshape(-1, TILE, TILE))  50.6 us
    dot_general x2, matrix products, local(): jnp.einsum('aip,bjp->abij', factor, column_factor, precision=lax.Precisio...  31.7 us
  transfers between devices with their start and end apart: 8, of which 7 were waited for; matrix products, arithmetic and copies ran while one was open for 5% of the time, Pallas kernels for 0%

profile of v1, /device:TPU:0, one launch (start us, length us, event | category | flops | bytes accessed | tf_op | source)
XLA Modules:
  0.0 1293.7 jit_solution(7627907448926578795)
XLA Ops:
  6.5 0.7 and_select_fusion.7
  7.9 0.7 select_reduce_fusion
  8.6 0.2 convert_reduce_fusion
  8.8 1.0 scatter_custom_fusion
  9.8 0.8 all_to_all.9
  10.6 11.1 all-to-all-start
  21.7 7.9 broadcast_in_dim.69
  29.6 23.7 %scatter_fusion = f32[256,128,128]{2,1,0:T(8,128)} fusion(f32[256,128,128]{2,1,0:T(8,128)} %broadcast_in_dim.69, s32[128]{0:T(128)S(1)} %fusion.16, f32[128,128,128]{2,1,0:T(8,128)} %bitcast.126), kind=kCustom, calls=%fused_computation.1 | custom fusion | bytes 25166336 | tf_op jit(solution)/shard_map/scatter | solution.py:54
  53.3 0.0 all-to-all-done
  53.3 10.5 all-to-all-start.1
  63.8 0.0 all-gather.13.cloned.1.call-start
  63.9 0.5 broadcast.445
  64.4 0.8 reduce.7
  65.2 0.1 reshape.347
  65.4 222.0 %all-to-all-done.1 = f32[128,2,128,128]{3,2,1,0:T(8,128)} async-done(((f32[128,2,128,128]{3,2,1,0:T(8,128)}), f32[128,2,128,128]{3,2,1,0:T(8,128)}, u32[]{:S(2)}, u32[]{:S(2)}) %all-to-all-start.1) | async-done | bytes 16777248 | tf_op jit(solution)/shard_map/all_to_all | solution.py:58
  287.4 4.5 broadcast_in_dim.64
  291.8 50.6 %scatter_fusion.1 = f32[128,128,128]{2,1,0:T(8,128)} fusion(f32[128,128,128]{2,1,0:T(8,128)} %broadcast_in_dim.64, s32[256]{0:T(256)S(1)} %bitcast.135, f32[256,128,128]{2,1,0:T(8,128)} %bitcast.11), kind=kCustom, calls=%fused_computation.2 | custom fusion | flops 4194304 | bytes 50332672 | tf_op jit(solution)/shard_map/scatter-add | solution.py:74
  342.4 1.9 slice_bitcast_fusion.1
  344.4 0.0 all-gather.13.cloned.1.call-update
  344.4 0.0 all-gather.17.cloned.1.call-start
  344.5 85.5 %all-gather.13.cloned.1.call-done = f32[64,1,128,128]{3,2,1,0:T(8,128)} async-done(((f32[8,1,128,128]{3,2,1,0:T(8,128)}), f32[64,1,128,128]{3,2,1,0:T(8,128)}) %all-gather.13.cloned.1.call-update) | async-done | bytes 4194320 | tf_op jit(solution)/shard_map/all_gather | solution.py:91
  430.0 0.0 slice-start
  430.0 1.6 slice-done
  431.6 1.4 copy.47
  432.9 1.9 dot_general.16
  434.9 7.4 broadcast_select_fusion.3
  442.3 0.0 all-gather.17.cloned.1.call-update
  442.3 0.0 all-gather.15.cloned.1.call-start
  442.4 0.7 all-gather.15.cloned.1.call-update
  443.1 11.8 all-gather.19.cloned.1.call-start
  454.9 7.7 copy.32
  462.6 0.9 bitcast_dynamic-update-slice_fusion.1
  463.5 147.3 %all-gather.17.cloned.1.call-done = f32[128,128,512]{2,1,0:T(8,128)} async-done(((f32[8,128,512]{2,1,0:T(8,128)}), f32[128,128,512]{2,1,0:T(8,128)}) %all-gather.17.cloned.1.call-update) | async-done | bytes 33554448 | tf_op jit(solution)/shard_map/all_gather | solution.py:16
  610.8 14.0 %reduce_sum.76 = f32[8,128,512]{2,1,0:T(8,128)} reduce(f32[16,8,128,512]{3,2,1,0:T(8,128)} %bitcast.122, f32[]{:T(128)} %constant.136.clone.1), dimensions={0}, to_apply=%region_7.8 | reduce | flops 7864320 | bytes 35651588 | tf_op jit(solution)/shard_map/reduce_sum | solution.py:16
  624.8 159.3 %all-gather.15.cloned.1.call-done = f32[128,128,512]{2,1,0:T(8,128)} async-done(((f32[8,128,512]{2,1,0:T(8,128)}), f32[128,128,512]{2,1,0:T(8,128)}) %all-gather.15.cloned.1.call-update) | async-done | bytes 33554448 | tf_op jit(solution)/shard_map/all_gather | solution.py:16
  784.1 14.1 %reduce_sum.75 = f32[8,128,512]{2,1,0:T(8,128)} reduce(f32[16,8,128,512]{3,2,1,0:T(8,128)} %bitcast.123, f32[]{:T(128)} %constant.136.clone.1), dimensions={0}, to_apply=%region_6.7 | reduce | flops 7864320 | bytes 35651588 | tf_op jit(solution)/shard_map/reduce_sum | solution.py:16
  798.2 2.7 pad_maximum_fusion
  800.9 16.6 %bitcast_subtract_fusion.1 = f32[8,16,128,128]{3,2,0,1:T(8,128)S(1)} fusion(f32[8,16,128,128]{3,2,0,1:T(8,128)} %bitcast_dynamic-update-slice_fusion.1, f32[16,128,512,1]{2,1,3,0:T(8,128)S(1)} %bitcast.124, f32[8,128,512]{2,1,0:T(8,128)S(1)} %get-tuple-element.43), kind=kOutput, calls=%fused_computation.5 | convolution fusion | flops 12886999040 | bytes 23068672 | tf_op jit(solution)/shard_map/aip,bjp->abij/dot_general | solution.py:108
  817.5 0.0 copy-start
  817.5 3.4 copy-done
  820.9 0.9 slice_bitcast_fusion
  821.8 0.0 all-gather.19.cloned.1.call-update
  821.8 0.0 all-gather.23.cloned.1.call-start
  821.9 72.6 %all-gather.19.cloned.1.call-done = f32[64,1,128,128]{3,2,1,0:T(8,128)} async-done(((f32[8,1,128,128]{3,2,1,0:T(8,128)}), f32[64,1,128,128]{3,2,1,0:T(8,128)}) %all-gather.19.cloned.1.call-update) | async-done | bytes 4194320 | tf_op jit(solution)/shard_map/all_gather | solution.py:91
  894.5 0.0 slice-start.1
  894.5 1.6 slice-done.1
  896.1 1.4 copy.46
  897.4 1.9 dot_general.19
  899.3 7.4 broadcast_select_fusion.1
  906.8 0.0 all-gather.23.cloned.1.call-update
  906.8 0.0 all-gather.21.cloned.1.call-start
  906.9 0.5 all-gather.21.cloned.1.call-update
  907.4 0.9 bitcast_dynamic-update-slice_fusion
  908.3 167.0 %all-gather.23.cloned.1.call-done = f32[128,128,512]{2,1,0:T(8,128)} async-done(((f32[8,128,512]{2,1,0:T(8,128)}), f32[128,128,512]{2,1,0:T(8,128)}) %all-gather.23.cloned.1.call-update) | async-done | bytes 33554448 | tf_op jit(solution)/shard_map/all_gather | solution.py:16
  1075.3 14.1 %reduce_sum.78 = f32[8,128,512]{2,1,0:T(8,128)} reduce(f32[16,8,128,512]{3,2,1,0:T(8,128)} %bitcast.120, f32[]{:T(128)} %constant.136.clone.1), dimensions={0}, to_apply=%region_9.10 | reduce | flops 7864320 | bytes 35651588 | tf_op jit(solution)/shard_map/reduce_sum | solution.py:16
  1089.5 159.0 %all-gather.21.cloned.1.call-done = f32[128,128,512]{2,1,0:T(8,128)} async-done(((f32[8,128,512]{2,1,0:T(8,128)}), f32[128,128,512]{2,1,0:T(8,128)}) %all-gather.21.cloned.1.call-update) | async-done | bytes 33554448 | tf_op jit(solution)/shard_map/all_gather | solution.py:16
  1248.5 14.2 %reduce_sum.77 = f32[8,128,512]{2,1,0:T(8,128)} reduce(f32[16,8,128,512]{3,2,1,0:T(8,128)} %bitcast.121, f32[]{:T(128)} %constant.136.clone.1), dimensions={0}, to_apply=%region_8.9 | reduce | flops 7864320 | bytes 35651588 | tf_op jit(solution)/shard_map/reduce_sum | solution.py:16
  1262.7 0.0 copy-start.1
  1262.7 3.1 pad_maximum_fusion.1
  1265.8 1.6 copy-done.1
  1267.3 15.1 %fusion = f32[8,1,16,1,128,128]{5,4,0,2,3,1:T(8,128)S(1)} fusion(f32[8,16,128,128]{3,2,0,1:T(8,128)S(1)} %copy-done.1, f32[16,128,512,1]{2,1,3,0:T(8,128)S(1)} %bitcast.125, f32[8,128,512]{2,1,0:T(8,128)S(1)} %get-tuple-element.44), kind=kOutput, calls=%fused_computation.4 | convolution fusion | flops 12886999040 | bytes 23068672 | tf_op jit(solution)/shard_map/aip,bjp->abij/dot_general | solution.py:108
  1282.4 4.0 copy.37
  (6 shorter events, 0.1 us)
Async XLA Ops:
  10.6 42.7 %all-to-all-start = ((s32[128,1,2]{2,1,0:T(1,128)}), s32[128,1,2]{2,1,0:T(1,128)S(1)}, u32[]{:S(2)}, u32[]{:S(2)}) async-start(s32[128,1,2]{2,1,0:T(1,128)} %bitcast.7), calls=%async_computation | async-start | bytes 131072 | tf_op jit(solution)/shard_map/all_to_all | solution.py:65
  53.3 234.0 %all-to-all-start.1 = ((f32[128,2,128,128]{3,2,1,0:T(8,128)}), f32[128,2,128,128]{3,2,1,0:T(8,128)}, u32[]{:S(2)}, u32[]{:S(2)}) async-start(f32[128,2,128,128]{3,2,1,0:T(8,128)} %bitcast.119), calls=%async_computation.1 | async-start | bytes 33554432 | tf_op jit(solution)/shard_map/all_to_all | solution.py:58
  63.8 366.2 %all-gather.13.cloned.1.call-start = ((), (), s32[]{:S(2)}) async-start(), calls=%async_computation.2 | async-start | bytes 4718592 | tf_op jit(solution)/shard_map/all_gather | solution.py:91
  344.4 266.4 %all-gather.17.cloned.1.call-start = ((), (), s32[]{:S(2)}) async-start(), calls=%async_computation.4 | async-start | bytes 35651584 | tf_op jit(solution)/shard_map/all_gather | solution.py:16
  430.0 1.6 slice-start
  442.3 341.8 %all-gather.15.cloned.1.call-start = ((), (), s32[]{:S(2)}) async-start(), calls=%async_computation.3 | async-start | bytes 35651584 | tf_op jit(solution)/shard_map/all_gather | solution.py:16
  443.1 451.4 %all-gather.19.cloned.1.call-start = ((), (), s32[]{:S(2)}) async-start(), calls=%async_computation.5 | async-start | bytes 4718592 | tf_op jit(solution)/shard_map/all_gather | solution.py:91
  817.5 3.4 copy-start
  821.8 253.5 %all-gather.23.cloned.1.call-start = ((), (), s32[]{:S(2)}) async-start(), calls=%async_computation.7 | async-start | bytes 35651584 | tf_op jit(solution)/shard_map/all_gather | solution.py:16
  894.5 1.6 slice-start.1
  906.8 341.6 %all-gather.21.cloned.1.call-start = ((), (), s32[]{:S(2)}) async-start(), calls=%async_computation.6 | async-start | bytes 35651584 | tf_op jit(solution)/shard_map/all_gather | solution.py:16
  1262.7 4.6 copy-start.1
Sparse Core Ops, SparseCore 0:
  344.5 85.4 all-gather.12
  442.4 168.3 all-gather.16
  612.5 171.5 all-gather.14
  821.9 72.5 all-gather.18
  906.9 168.3 all-gather.22
  1076.9 171.5 all-gather.20
